TPU v7x, 32 devices: a whole 2x2x4 slice. The times are simulated.
32 devices in a mesh: dp: 8 (over z, y), fsdp: 4 (over x, core).
Axes of the slice: x: 2, y: 2, z: 4, core: 2. Of those that a mesh axis runs over, the one named last changes fastest.
Arguments:
- picture_tower_inputs: bfloat16 [16384, 1152], P(('dp', 'fsdp')), may hold values from -6 to 6
- caption_tower_inputs: bfloat16 [16384, 1152], P(('dp', 'fsdp')), may hold values from -6 to 6
- halfwidth_parameter_matrix: bfloat16 [1152, 2304], P('fsdp'), may hold values from -0.1875 to 0.1875
- affinity_multiplier: float32 [1], replicated, may hold values from 4 to 12
- affinity_offset: float32 [1], replicated, may hold values from -6 to -2
- precise_parameter_copy: float32 [1152, 2304], P('fsdp', 'dp'), may hold values from -0.125 to 0.125
- gradient_mean_estimate: float32 [1152, 2304], P('fsdp', 'dp'), may hold values from -4 to 4
- gradient_variance_estimate: float32 [1152, 2304], P('fsdp', 'dp'), may hold values from 0.05 to 1
Outputs:
- img_tangent: bfloat16 [16384, 1152], P(('dp', 'fsdp'))
- txt_tangent: bfloat16 [16384, 1152], P(('dp', 'fsdp'))
- new_master: float32 [1152, 2304], P('fsdp', 'dp')
- new_one: float32 [1152, 2304], P('fsdp', 'dp')
- new_two: float32 [1152, 2304], P('fsdp', 'dp')
- new_weights: bfloat16 [1152, 2304], P('fsdp')
All inputs are finite; a program needn't handle non-finite values.
Results may differ from a plain program's by a relative error of at most 0.008.
Values may be sent and summed in bfloat16 or wider, within the bound.
A program may use at most 128 MiB of HBM per device.

v0:
```python
import jax
import jax.numpy as jnp
from jax import lax
from jax.sharding import PartitionSpec as P

CYCLE = 4


def shifted(value, axis, steps):
    count = lax.axis_size(axis)
    pairs = [(source, (source + steps) % count) for source in range(count)]
    return lax.ppermute(value, axis, pairs)


def normalize(projected):
    inv_norm = lax.rsqrt(jnp.sum(projected * projected, axis=-1, keepdims=True) + 1e-06)
    return (projected * inv_norm, inv_norm)


def contract_rows(left, right):
    return lax.dot_general(
        left, right, (((0,), (0,)), ((), ())), preferred_element_type=jnp.float32
    )


def weigh_pairs(image_rows, text_rows, affinity_multiplier_name, shift_value, sign_label):
    logits = (
        affinity_multiplier_name
        * lax.dot_general(
            image_rows, text_rows, (((1,), (1,)), ((), ())), preferred_element_type=jnp.float32
        )
        + shift_value
    )
    return (-sign_label * jax.nn.sigmoid(-sign_label * logits) * affinity_multiplier_name).astype(
        jnp.bfloat16
    )


def body(
    picture_tower_inputs,
    caption_tower_inputs,
    halfwidth_parameter_matrix,
    affinity_multiplier,
    affinity_offset,
    precise_parameter_copy,
    gradient_mean_estimate,
    gradient_variance_estimate,
):
    row_count = picture_tower_inputs.shape[0]
    feature_width = picture_tower_inputs.shape[1]
    zero_block = jnp.zeros((row_count, feature_width), jnp.float32)
    rows_per_block = lax.all_gather(halfwidth_parameter_matrix, "fsdp", axis=0, tiled=True)
    part_img = picture_tower_inputs
    part_txt = caption_tower_inputs
    proj_img = jnp.dot(
        part_img, rows_per_block[:, :feature_width], preferred_element_type=jnp.float32
    )
    proj_txt = jnp.dot(
        part_txt, rows_per_block[:, feature_width:], preferred_element_type=jnp.float32
    )
    unit_img, norm_img = normalize(proj_img)
    normalized_text, norm_txt = normalize(proj_txt)
    low_img = unit_img.astype(jnp.bfloat16)
    low_txt = normalized_text.astype(jnp.bfloat16)
    affinity_multiplier_name = affinity_multiplier[0]
    shift_value = affinity_offset[0]
    identity_mask = jnp.eye(row_count, dtype=jnp.float32)
    negative_label = -jnp.ones_like(identity_mask)
    visiting = low_txt
    carried = zero_block
    grad_img = zero_block
    for cycle_step in range(CYCLE):
        if cycle_step > 0:
            visiting = shifted(visiting, "dp", 1)
            carried = shifted(carried, "dp", 1)
        if cycle_step == 0:
            sign_label = 2.0 * identity_mask - 1.0
        else:
            sign_label = negative_label
        pair_weight = weigh_pairs(
            low_img, visiting, affinity_multiplier_name, shift_value, sign_label
        )
        grad_img = grad_img + jnp.dot(pair_weight, visiting, preferred_element_type=jnp.float32)
        carried = carried + contract_rows(pair_weight, low_img)
    grad_txt = shifted(carried, "dp", 1 - CYCLE)
    img_tangent = (
        norm_img * (grad_img - unit_img * jnp.sum(unit_img * grad_img, axis=1, keepdims=True))
    ).astype(jnp.bfloat16)
    txt_tangent = (
        norm_txt
        * (grad_txt - normalized_text * jnp.sum(normalized_text * grad_txt, axis=1, keepdims=True))
    ).astype(jnp.bfloat16)
    part_img = picture_tower_inputs
    part_txt = caption_tower_inputs
    owned_rows = lax.psum_scatter(
        jnp.concatenate(
            [contract_rows(part_img, img_tangent), contract_rows(part_txt, txt_tangent)], axis=1
        ).astype(jnp.bfloat16),
        "fsdp",
        scatter_dimension=0,
        tiled=True,
    ).astype(jnp.float32)
    gradient = lax.psum_scatter(owned_rows, "dp", scatter_dimension=1, tiled=True)
    new_one = 0.9 * gradient_mean_estimate + 0.1 * gradient
    new_two = 0.95 * gradient_variance_estimate + 0.05 * gradient * gradient
    new_master = precise_parameter_copy - 0.001 * (
        new_one / (jnp.sqrt(new_two) + 1e-08) + 0.1 * precise_parameter_copy
    )
    new_weights = lax.all_gather(new_master.astype(jnp.bfloat16), "dp", axis=1, tiled=True)
    return (img_tangent, txt_tangent, new_master, new_one, new_two, new_weights)


def solution(mesh):
    return jax.shard_map(
        body,
        mesh=mesh,
        in_specs=(
            P(("dp", "fsdp"), None),
            P(("dp", "fsdp"), None),
            P("fsdp", None),
            P(),
            P(),
            P("fsdp", "dp"),
            P("fsdp", "dp"),
            P("fsdp", "dp"),
        ),
        out_specs=(
            P(("dp", "fsdp"), None),
            P(("dp", "fsdp"), None),
            P("fsdp", "dp"),
            P("fsdp", "dp"),
            P("fsdp", "dp"),
            P("fsdp", None),
        ),
        check_vma=False,
    )
```

profile of v0, /device:TPU:0, one launch (start us, length us, event | category | flops | bytes accessed | tf_op | source)
XLA Modules:
  0.0 615.6 jit_solution(11940771323395554887)
XLA Ops:
  7.2 0.7 all-gather.3.cloned.1.call-update
  9.3 43.8 %all-gather.3.cloned.1.call-done = bf16[1152,2304]{1,0:T(8,128)(2,1)} async-done(((bf16[288,2304]{1,0:T(8,128)(2,1)}), bf16[1152,2304]{1,0:T(8,128)(2,1)}) %all-gather.3.cloned.1.call-update) | async-done | bytes 5308432 | tf_op jit(solution)/shard_map/all_gather | solution.py:52
  53.1 3.8 multiply_reduce_fusion.3
  57.0 1.9 multiply_reduce_fusion.2
  58.9 0.2 multiply_convert_fusion.3
  59.3 1.1 fusion.32
  60.4 0.9 fusion.40
  61.3 1.5 collective-permute-start.3
  62.8 1.5 collective-permute-start
  64.3 78.4 %collective-permute-done = bf16[512,1152]{1,0:T(8,128)(2,1)S(1)} collective-permute-done((bf16[512,1152]{1,0:T(8,128)(2,1)S(1)}, bf16[512,1152]{1,0:T(8,128)(2,1)S(1)}, u32[]{:S(2)}, u32[]{:S(2)}) %collective-permute-start) | collective-permute-done | bytes 1179680 | tf_op jit(solution)/shard_map/ppermute | solution.py:12
  142.7 1.0 fusion.35
  143.8 0.9 convolution_add_fusion
  144.7 1.1 collective-permute-start.1
  145.9 79.4 %collective-permute-done.1 = bf16[512,1152]{1,0:T(8,128)(2,1)S(1)} collective-permute-done((bf16[512,1152]{1,0:T(8,128)(2,1)S(1)}, bf16[512,1152]{1,0:T(8,128)(2,1)S(1)}, u32[]{:S(2)}, u32[]{:S(2)}) %collective-permute-start.1) | collective-permute-done | bytes 1179680 | tf_op jit(solution)/shard_map/ppermute | solution.py:12
  225.3 1.0 fusion.34
  226.3 0.9 fusion.41
  227.2 0.2 add.99
  227.5 79.7 %collective-permute-done.2 = bf16[512,1152]{1,0:T(8,128)(2,1)S(1)} collective-permute-done((bf16[512,1152]{1,0:T(8,128)(2,1)S(1)}, bf16[512,1152]{1,0:T(8,128)(2,1)S(1)}, u32[]{:S(2)}, u32[]{:S(2)}) %collective-permute-start.2) | collective-permute-done | bytes 1179680 | tf_op jit(solution)/shard_map/ppermute | solution.py:12
  307.2 1.0 fusion.33
  308.2 0.9 fusion.42
  309.1 0.2 add.100
  309.4 0.2 collective-permute-start.6
  309.6 0.8 fusion.39
  310.5 0.8 convolution_add_fusion.3
  311.3 0.9 convolution_add_fusion.2
  312.2 1.1 multiply_reduce_fusion.1
  313.3 0.4 multiply_convert_fusion.1
  313.7 1.7 fusion
  315.5 45.6 %collective-permute-done.6 = f32[512,1152]{1,0:T(8,128)S(1)} collective-permute-done((f32[512,1152]{1,0:T(8,128)S(1)}, f32[512,1152]{1,0:T(8,128)S(1)}, u32[]{:S(2)}, u32[]{:S(2)}) %collective-permute-start.6) | collective-permute-done | bytes 2359328 | tf_op jit(solution)/shard_map/ppermute | solution.py:12
  361.1 0.4 multiply_reduce_fusion
  361.5 0.4 multiply_convert_fusion
  361.9 1.0 copy-done.2
  363.0 1.7 fusion.1
  364.7 2.8 pad_maximum_fusion
  367.5 8.6 %copy.30 = bf16[1152,2304]{1,0:T(8,128)(2,1)} copy(bf16[1152,2304]{0,1:T(8,128)(2,1)} %pad_maximum_fusion) | data formatting | bytes 10616832
  376.1 98.7 %reduce-scatter.7.cloned.1.call-done = bf16[288,2304]{1,0:T(8,128)(2,1)} async-done(((bf16[1152,2304]{1,0:T(8,128)(2,1)}), bf16[288,2304]{1,0:T(8,128)(2,1)}) %reduce-scatter.7.cloned.1.call-update) | async-done | bytes 1327120
  474.8 1.9 copy.31
  476.7 2.0 convert_element_type.40
  478.8 0.9 copy-done.3
  479.9 0.2 copy.23
  480.2 1.0 copy.22
  481.1 77.0 %reduce-scatter.5.cloned.1.call-done = f32[288,288]{0,1:T(8,128)} async-done(((f32[288,2304]{0,1:T(8,128)}), f32[288,288]{0,1:T(8,128)}) %reduce-scatter.5.cloned.1.call-update) | async-done | bytes 331792 | tf_op jit(solution)/shard_map/reduce_scatter | solution.py:103
  558.1 2.2 fusion.37
  560.3 1.0 copy.26
  561.3 1.0 copy.27
  562.3 1.0 copy.28
  563.2 43.2 %all-gather.5.cloned.1.call-done = bf16[288,2304]{0,1:T(8,128)(2,1)} async-done(((bf16[288,288]{0,1:T(8,128)(2,1)}), bf16[288,2304]{0,1:T(8,128)(2,1)}) %all-gather.5.cloned.1.call-update) | async-done | bytes 1327120 | tf_op jit(solution)/shard_map/all_gather | solution.py:109
  606.5 2.6 copy.29
  (31 shorter events, 0.8 us)
Async XLA Ops:
  7.2 45.9 %copy-start = (bf16[512,1152]{1,0:T(8,128)(2,1)S(1)}, bf16[512,1152]{1,0:T(8,128)(2,1)}, u32[]{:S(2)}) copy-start(bf16[512,1152]{1,0:T(8,128)(2,1)} %param.8) | copy-start | bytes 3538948
  7.2 45.9 %all-gather.3.cloned.1.call-start = ((), (), s32[]{:S(2)}) async-start(), calls=%async_computation.2 | async-start | bytes 6635520 | tf_op jit(solution)/shard_map/all_gather | solution.py:52
  7.9 466.9 %reduce-scatter.7.cloned.1.call-start = ((), (), s32[]{:S(2)}) async-start(), calls=%async_computation.5 | async-start | bytes 6635520
  9.3 47.7 %copy-start.7 = (bf16[512,1152]{1,0:T(8,128)(2,1)S(1)}, bf16[512,1152]{1,0:T(8,128)(2,1)}, u32[]{:S(2)}) copy-start(bf16[512,1152]{1,0:T(8,128)(2,1)} %param.9) | copy-start | bytes 3538948
  53.1 3.9 copy-start.6
  61.3 82.5 %collective-permute-start.3 = (f32[512,1152]{1,0:T(8,128)S(1)}, f32[512,1152]{1,0:T(8,128)S(1)}, u32[]{:S(2)}, u32[]{:S(2)}) collective-permute-start(f32[512,1152]{1,0:T(8,128)S(1)} %fusion.40), channel_id=1, source_target_pairs={{0,4},{4,8},{8,12},{12,16},{16,20},{20,24},{24,28},{28,0},{1,5},{5... | collective-permute-start | bytes 7077896 | tf_op jit(solution)/shard_map/ppermute | solution.py:12
  62.8 79.9 %collective-permute-start = (bf16[512,1152]{1,0:T(8,128)(2,1)S(1)}, bf16[512,1152]{1,0:T(8,128)(2,1)S(1)}, u32[]{:S(2)}, u32[]{:S(2)}) collective-permute-start(bf16[512,1152]{1,0:T(8,128)(2,1)S(1)} %multiply_convert_fusion.2), channel_id=1, source_target_pairs={{0,4},{4,8},{8,12},{12,16},{16,20},{20,24},{24,28},{28,0},{1,5},{5... | collective-permute-start | bytes 3538952 | tf_op jit(solution)/shard_map/ppermute | solution.py:12
  144.6 82.5 %collective-permute-start.4 = (f32[512,1152]{1,0:T(8,128)S(1)}, f32[512,1152]{1,0:T(8,128)S(1)}, u32[]{:S(2)}, u32[]{:S(2)}) collective-permute-start(f32[512,1152]{1,0:T(8,128)S(1)} %convolution_add_fusion), channel_id=1, source_target_pairs={{0,4},{4,8},{8,12},{12,16},{16,20},{20,24},{24,28},{28,0},{1,5},{5... | collective-permute-start | bytes 7077896 | tf_op jit(solution)/shard_map/ppermute | solution.py:12
  144.7 80.5 %collective-permute-start.1 = (bf16[512,1152]{1,0:T(8,128)(2,1)S(1)}, bf16[512,1152]{1,0:T(8,128)(2,1)S(1)}, u32[]{:S(2)}, u32[]{:S(2)}) collective-permute-start(bf16[512,1152]{1,0:T(8,128)(2,1)S(1)} %collective-permute-done), channel_id=1, source_target_pairs={{0,4},{4,8},{8,12},{12,16},{16,20},{20,24},{24,28},{28,0},{1,5},{5... | collective-permute-start | bytes 3538952 | tf_op jit(solution)/shard_map/ppermute | solution.py:12
  227.4 81.7 %collective-permute-start.5 = (f32[512,1152]{1,0:T(8,128)S(1)}, f32[512,1152]{1,0:T(8,128)S(1)}, u32[]{:S(2)}, u32[]{:S(2)}) collective-permute-start(f32[512,1152]{1,0:T(8,128)S(1)} %add.99), channel_id=1, source_target_pairs={{0,4},{4,8},{8,12},{12,16},{16,20},{20,24},{24,28},{28,0},{1,5},{5... | collective-permute-start | bytes 7077896 | tf_op jit(solution)/shard_map/ppermute | solution.py:12
  227.5 79.7 %collective-permute-start.2 = (bf16[512,1152]{1,0:T(8,128)(2,1)S(1)}, bf16[512,1152]{1,0:T(8,128)(2,1)S(1)}, u32[]{:S(2)}, u32[]{:S(2)}) collective-permute-start(bf16[512,1152]{1,0:T(8,128)(2,1)S(1)} %collective-permute-done.1), channel_id=1, source_target_pairs={{0,4},{4,8},{8,12},{12,16},{16,20},{20,24},{24,28},{28,0},{1,5},{5... | collective-permute-start | bytes 3538952 | tf_op jit(solution)/shard_map/ppermute | solution.py:12
  309.4 51.8 %collective-permute-start.6 = (f32[512,1152]{1,0:T(8,128)S(1)}, f32[512,1152]{1,0:T(8,128)S(1)}, u32[]{:S(2)}, u32[]{:S(2)}) collective-permute-start(f32[512,1152]{1,0:T(8,128)S(1)} %add.100), channel_id=1, source_target_pairs={{0,20},{4,24},{8,28},{12,0},{16,4},{20,8},{24,12},{28,16},{1,21},{... | collective-permute-start | bytes 7077896 | tf_op jit(solution)/shard_map/ppermute | solution.py:12
  313.7 1.8 copy-start.1
  361.9 1.0 copy-start.2
  376.1 182.1 %reduce-scatter.5.cloned.1.call-start = ((), (), s32[]{:S(2)}) async-start(), calls=%async_computation.3 | async-start | bytes 3981312 | tf_op jit(solution)/shard_map/reduce_scatter | solution.py:103
  478.7 1.0 copy-start.3
  478.7 1.2 copy-start.4
  478.7 1.4 copy-start.5
  478.8 127.7 %all-gather.5.cloned.1.call-start = ((), (), s32[]{:S(2)}) async-start(), calls=%async_computation.4 | async-start | bytes 1990656 | tf_op jit(solution)/shard_map/all_gather | solution.py:109
Sparse Core Ops, SparseCore 0:
  9.6 43.4 all-gather.2
  376.2 98.5 reduce-scatter.6
  478.9 79.2 reduce-scatter.4
  561.0 45.4 all-gather.4
where the time goes:
time: 616 us
  waiting for transfers between devices  547 us (89%)
  matrix products  20.5 us (3%)
  local copies, waits for them, and re-layouts  19.3 us (3%)
  between operations  15.3 us (2%)
  other arithmetic  9.06 us (1%)
    ppermute x7, waiting for transfers between devices, shifted(): return lax.ppermute(value, axis, pairs)  283 us
    unnamed x5, waiting for transfers between devices  99.4 us
    reduce_scatter x1, waiting for transfers between devices, body(): lax.psum_scatter(owned_rows, 'dp', scatter_dimension=1, tiled=True)  77 us
    all_gather x1, waiting for transfers between devices, body(): lax.all_gather(halfwidth_parameter_matrix, 'fsdp', axis=0, tiled=True)  43.8 us
    all_gather x1, waiting for transfers between devices, body(): lax.all_gather(new_master.astype(jnp.bfloat16), 'dp', axis=1, tiled=True)  43.2 us
    unnamed x25, local copies, waits for them, and re-layouts  19.3 us
  transfers between devices with their start and end apart: 11, of which 8 were waited for; matrix products, arithmetic and copies ran while one was open for 2% of the time, Pallas kernels for 0%

commit v1 on v0

v1 whole, which is shorter than its diff:
```python
import jax
import jax.numpy as jnp
from jax import lax
from jax.sharding import PartitionSpec as P

CYCLE = 4


def shifted(value, axis, steps):
    count = lax.axis_size(axis)
    pairs = [(source, (source + steps) % count) for source in range(count)]
    return lax.ppermute(value, axis, pairs)


def swapped(value, axis, bit):
    count = lax.axis_size(axis)
    return lax.ppermute(value, axis, [(source, source ^ bit) for source in range(count)])


def bit_of(axis, bit):
    return (lax.axis_index(axis) // bit) % 2 == 1


def ordered(mine, other, high):
    return jnp.where(high, other, mine), jnp.where(high, mine, other)


def normalize(projected):
    inv_norm = lax.rsqrt(jnp.sum(projected * projected, axis=-1, keepdims=True) + 1e-06)
    return (projected * inv_norm, inv_norm)


def contract_rows(left, right):
    return lax.dot_general(
        left, right, (((0,), (0,)), ((), ())), preferred_element_type=jnp.float32
    )


def weigh_pairs(left, right, scale, shift, sign_label):
    logits = (
        scale
        * lax.dot_general(
            left, right, (((1,), (1,)), ((), ())), preferred_element_type=jnp.float32
        )
        + shift
    )
    return (-sign_label * jax.nn.sigmoid(-sign_label * logits) * scale).astype(jnp.bfloat16)


def gather_weights(shard):
    rows = shard.shape[0]
    half = rows // 2
    y = bit_of("dp", 1)
    x = bit_of("fsdp", 2)
    c = bit_of("fsdp", 1)
    mine = jnp.where(y, shard[half:], shard[:half])
    got = swapped(mine, "fsdp", 2)
    rest = swapped(got, "dp", 1)
    low, high = ordered(got, rest, y)
    remote = jnp.concatenate([low, high], axis=0)
    own_core = swapped(shard, "fsdp", 1)
    remote_core = swapped(remote, "fsdp", 1)
    own_pair = jnp.concatenate(ordered(shard, own_core, c), axis=0)
    remote_pair = jnp.concatenate(ordered(remote, remote_core, c), axis=0)
    return jnp.concatenate(ordered(own_pair, remote_pair, x), axis=0)


def tangent(inv_norm, unit, grad):
    return (inv_norm * (grad - unit * jnp.sum(unit * grad, axis=1, keepdims=True))).astype(
        jnp.bfloat16
    )


def reduce_half(value, dim, axis, bit):
    high = bit_of(axis, bit)
    low_half = lax.index_in_dim(value, 0, dim, keepdims=False)
    high_half = lax.index_in_dim(value, 1, dim, keepdims=False)
    send = jnp.where(high, low_half, high_half).astype(jnp.bfloat16)
    keep = jnp.where(high, high_half, low_half).astype(jnp.float32)
    return keep + swapped(send, axis, bit).astype(jnp.float32)


def body(
    picture_tower_inputs,
    caption_tower_inputs,
    halfwidth_parameter_matrix,
    affinity_multiplier,
    affinity_offset,
    precise_parameter_copy,
    gradient_mean_estimate,
    gradient_variance_estimate,
):
    row_count, width = picture_tower_inputs.shape
    n_dp = lax.axis_size("dp")
    scale = affinity_multiplier[0]
    shift = affinity_offset[0]

    weights_img = gather_weights(halfwidth_parameter_matrix[:, :width])
    weights_txt = gather_weights(halfwidth_parameter_matrix[:, width:])
    unit_img, norm_img = normalize(
        jnp.dot(picture_tower_inputs, weights_img, preferred_element_type=jnp.float32)
    )
    unit_txt, norm_txt = normalize(
        jnp.dot(caption_tower_inputs, weights_txt, preferred_element_type=jnp.float32)
    )
    low_img = unit_img.astype(jnp.bfloat16)
    low_txt = unit_txt.astype(jnp.bfloat16)

    diagonal = 2.0 * jnp.eye(row_count, dtype=jnp.float32) - 1.0
    pair_weight = weigh_pairs(low_img, low_txt, scale, shift, diagonal)
    grad_img = jnp.dot(pair_weight, low_txt, preferred_element_type=jnp.float32)
    grad_txt = contract_rows(pair_weight, low_img)
    visiting_txt, visiting_img = low_txt, low_img
    for _ in range(1, CYCLE):
        visiting_img = shifted(visiting_img, "dp", -1)
        visiting_txt = shifted(visiting_txt, "dp", 1)
        of_img = weigh_pairs(low_img, visiting_txt, scale, shift, -1.0)
        of_txt = weigh_pairs(low_txt, visiting_img, scale, shift, -1.0)
        grad_img = grad_img + jnp.dot(of_img, visiting_txt, preferred_element_type=jnp.float32)
        grad_txt = grad_txt + jnp.dot(of_txt, visiting_img, preferred_element_type=jnp.float32)
    img_tangent = tangent(norm_img, unit_img, grad_img)
    txt_tangent = tangent(norm_txt, unit_txt, grad_txt)

    owned = 2 * width // n_dp
    piece = width // 2
    pieces = []
    for y in range(2):
        for features, rows in (
            (picture_tower_inputs, img_tangent),
            (caption_tower_inputs, txt_tangent),
        ):
            columns = rows.reshape(row_count, n_dp // 4, 2, owned)[:, :, y].reshape(row_count, piece)
            pieces.append(contract_rows(features, columns).astype(jnp.bfloat16))
    shard_rows = width // lax.axis_size("fsdp")
    half = shard_rows // 2
    split = [p.reshape(2, 2, 2, half, piece) for p in pieces]

    new_parts = []
    for part in range(2):
        total = jnp.stack([s[:, :, part] for s in split]).reshape(2, 2, 2, 2, half, piece)
        total = reduce_half(total, 3, "fsdp", 1)
        if part == 0:
            total = reduce_half(total, 2, "fsdp", 2)
            total = reduce_half(total, 0, "dp", 1)
        else:
            total = reduce_half(total, 0, "dp", 1)
            total = reduce_half(total, 1, "fsdp", 2)
        total = reduce_half(total, 0, "dp", n_dp // 2)
        bit = n_dp // 4
        while bit > 1:
            size = total.shape[-1] // 2
            total = reduce_half(jnp.stack([total[:, :size], total[:, size:]]), 0, "dp", bit)
            bit //= 2
        rows = slice(part * half, (part + 1) * half)
        new_one = 0.9 * gradient_mean_estimate[rows] + 0.1 * total
        new_two = 0.95 * gradient_variance_estimate[rows] + 0.05 * total * total
        master = precise_parameter_copy[rows]
        new_master = master - 0.001 * (new_one / (jnp.sqrt(new_two) + 1e-08) + 0.1 * master)

        gathered = new_master.astype(jnp.bfloat16)[None]
        bit = n_dp // 2
        order = []
        while bit >= 1:
            other = swapped(gathered, "dp", bit)
            gathered = jnp.concatenate(ordered(gathered, other, bit_of("dp", bit)), axis=0)
            order.append(bit)
            bit //= 2
        bits = len(order)
        gathered = gathered.reshape((2,) * bits + (half, owned))
        gathered = gathered.transpose((bits,) + tuple(reversed(range(bits))) + (bits + 1,))
        new_parts.append((new_master, new_one, new_two, gathered.reshape(half, 2 * width)))
    new_master, new_one, new_two, new_weights = (
        jnp.concatenate(both, axis=0) for both in zip(*new_parts)
    )
    return (img_tangent, txt_tangent, new_master, new_one, new_two, new_weights)


def solution(mesh):
    return jax.shard_map(
        body,
        mesh=mesh,
        in_specs=(
            P(("dp", "fsdp"), None),
            P(("dp", "fsdp"), None),
            P("fsdp", None),
            P(),
            P(),
            P("fsdp", "dp"),
            P("fsdp", "dp"),
            P("fsdp", "dp"),
        ),
        out_specs=(
            P(("dp", "fsdp"), None),
            P(("dp", "fsdp"), None),
            P("fsdp", "dp"),
            P("fsdp", "dp"),
            P("fsdp", "dp"),
            P("fsdp", None),
        ),
        check_vma=False,
    )
```

time: 616 us -> 346 us (0.56)
  waiting for transfers between devices: 547 us -> 196 us
  matrix products: 20.5 us -> 53.1 us
  starting transfers between devices: 4.71 us -> 34.6 us
  other arithmetic: 9.06 us -> 28 us
  between operations: 15.3 us -> 2.64 us
  local copies, waits for them, and re-layouts: 19.3 us -> 30 us
    ppermute x7 -> x6, waiting for transfers between devices: 283 us -> 117 us  [shifted(): return lax.ppermute(value, axis, pairs)]
    unnamed x5 -> x0, waiting for transfers between devices: 99.4 us -> none
    all_gather x2 -> x0, waiting for transfers between devices: 87.1 us -> none  [the longest x1 43.8 us: body(): lax.all_gather(halfwidth_parameter_matrix, 'fsdp', axis=0, tiled=True)]
    ppermute x0 -> x24, waiting for transfers between devices: none -> 79.2 us  [swapped(): lax.ppermute(value, axis, [(source, source ^ bit) for source in range(cou...]
    reduce_scatter x1 -> x0, waiting for transfers between devices: 77 us -> none  [body(): lax.psum_scatter(owned_rows, 'dp', scatter_dimension=1, tiled=True)]
    dot_general x10, matrix products: 13.5 us -> 42.9 us  [the longest x3 18.5 us: body(): jnp.dot(of_txt, visiting_img, preferred_element_type=jnp.float32)]
    ppermute x0 -> x24, starting transfers between devices: none -> 25.1 us  [swapped(): lax.ppermute(value, axis, [(source, source ^ bit) for source in range(cou...]
    convert_element_type x0 -> x4, local copies, waits for them, and re-layouts: none -> 8.39 us  [body(): pieces.append(contract_rows(features, columns).astype(jnp.bfloat16))]
  transfers between devices with their start and end apart: 11 -> 30, of which waited for: 8 -> 22; matrix products, arithmetic and copies ran while one was open for 2% -> 22% of each run, Pallas kernels for 0% -> 0%
where the time goes in v1:
time: 346 us; the launch traced here: 345 us
  waiting for transfers between devices  196 us (57%)
  matrix products  53.1 us (15%)
  starting transfers between devices  34.6 us (10%)
  local copies, waits for them, and re-layouts  30 us (9%)
  other arithmetic  28 us (8%)
    ppermute x6, waiting for transfers between devices, shifted(): return lax.ppermute(value, axis, pairs)  117 us
    ppermute x24, waiting for transfers between devices, swapped(): lax.ppermute(value, axis, [(source, source ^ bit) for source in range(cou...  79.2 us
    ppermute x24, starting transfers between devices, swapped(): lax.ppermute(value, axis, [(source, source ^ bit) for source in range(cou...  25.1 us
    dot_general x3, matrix products, body(): jnp.dot(of_txt, visiting_img, preferred_element_type=jnp.float32)  18.5 us
    dot_general x3, matrix products, body(): jnp.dot(of_img, visiting_txt, preferred_element_type=jnp.float32)  17.6 us
    unnamed x60, local copies, waits for them, and re-layouts  12.1 us
    dot_general x5, matrix products, contract_rows(): lax.dot_general(left, right, (((0,), (0,)), ((), ())), preferred_element_...  10.2 us
    ppermute x6, starting transfers between devices, shifted(): return lax.ppermute(value, axis, pairs)  9.53 us
  transfers between devices with their start and end apart: 30, of which 22 were waited for; matrix products, arithmetic and copies ran while one was open for 22% of the time, Pallas kernels for 0%

profile of v1, /device:TPU:0, one launch (start us, length us, event | category | flops | bytes accessed | tf_op | source)
XLA Modules:
  0.0 344.7 jit_solution(12502374392188680363)
XLA Ops:
  0.7 1.5 slice_select_fusion
  2.2 3.0 collective-permute-start.4
  5.3 8.7 %collective-permute-done.4 = bf16[144,1152]{1,0:T(8,128)(2,1)} collective-permute-done((bf16[144,1152]{1,0:T(8,128)(2,1)S(1)}, bf16[144,1152]{1,0:T(8,128)(2,1)}, u32[]{:S(2)}, u32[]{:S(2)}) %collective-permute-start.4) | collective-permute-done | bytes 331808 | tf_op jit(solution)/shard_map/ppermute | solution.py:17
  13.9 2.1 collective-permute-start.5
  16.9 3.3 collective-permute-done
  20.2 1.8 collective-permute-start.1
  23.7 5.7 %collective-permute-done.1 = bf16[144,1152]{1,0:T(8,128)(2,1)S(1)} collective-permute-done((bf16[144,1152]{1,0:T(8,128)(2,1)}, bf16[144,1152]{1,0:T(8,128)(2,1)S(1)}, u32[]{:S(2)}, u32[]{:S(2)}) %collective-permute-start.1) | collective-permute-done | bytes 331808 | tf_op jit(solution)/shard_map/ppermute | solution.py:17
  32.1 1.8 multiply_reduce_fusion
  35.9 1.8 multiply_reduce_fusion.1
  38.0 4.5 %collective-permute-start.11 = (bf16[512,1152]{0,1:T(8,128)(2,1)S(1)}, bf16[512,1152]{0,1:T(8,128)(2,1)}, u32[]{:S(2)}, u32[]{:S(2)}) collective-permute-start(bf16[512,1152]{0,1:T(8,128)(2,1)S(1)} %bitcast_convert_fusion.1), channel_id=1, source_target_pairs={{0,28},{4,0},{8,4},{12,8},{16,12},{20,16},{24,20},{28,24},{1,29},{... | collective-permute-start | bytes 3538952 | tf_op jit(solution)/shard_map/ppermute | solution.py:12
  45.4 46.0 %collective-permute-done.11 = bf16[512,1152]{0,1:T(8,128)(2,1)} collective-permute-done((bf16[512,1152]{0,1:T(8,128)(2,1)S(1)}, bf16[512,1152]{0,1:T(8,128)(2,1)}, u32[]{:S(2)}, u32[]{:S(2)}) %collective-permute-start.11) | collective-permute-done | bytes 1179680 | tf_op jit(solution)/shard_map/ppermute | solution.py:12
  91.4 2.4 collective-permute-start.12
  93.8 2.2 fusion.115
  96.0 2.2 fusion.114
  98.3 5.9 %convolution_add_fusion.2 = f32[512,1152]{0,1:T(8,128)} fusion(f32[512,1152]{0,1:T(8,128)} %fusion.115, bf16[512,1152]{0,1:T(8,128)(2,1)} %collective-permute-done.11, bf16[512,1152]{0,1:T(8,128)(2,1)} %copy-done.13, f32[]{:T(128)} %bitcast.179, f32[]{:T(128)} %bitcast.172), kind=kOutput, calls=%fused_computation.2 | convolution fusion | flops 1210384384 | bytes 7077896 | tf_op jit(solution)/shard_map/dot_general | solution.py:120
  104.2 39.8 %collective-permute-done.12 = bf16[512,1152]{0,1:T(8,128)(2,1)} collective-permute-done((bf16[512,1152]{0,1:T(8,128)(2,1)}, bf16[512,1152]{0,1:T(8,128)(2,1)}, u32[]{:S(2)}, u32[]{:S(2)}) %collective-permute-start.12) | collective-permute-done | bytes 1179680 | tf_op jit(solution)/shard_map/ppermute | solution.py:12
  144.0 2.5 collective-permute-start.13
  146.5 5.9 %convolution_add_fusion.5 = f32[512,1152]{0,1:T(8,128)} fusion(f32[512,1152]{0,1:T(8,128)} %fusion.114, bf16[512,1152]{0,1:T(8,128)(2,1)} %collective-permute-done.8, bf16[512,1152]{0,1:T(8,128)(2,1)} %copy-done.10, f32[]{:T(128)} %bitcast.182, f32[]{:T(128)} %bitcast.173), kind=kOutput, calls=%fused_computation.5 | convolution fusion | flops 1210384384 | bytes 7077896 | tf_op jit(solution)/shard_map/dot_general | solution.py:119
  152.5 5.9 %convolution_add_fusion.1 = f32[512,1152]{0,1:T(8,128)} fusion(f32[512,1152]{0,1:T(8,128)} %convolution_add_fusion.2, bf16[512,1152]{0,1:T(8,128)(2,1)} %collective-permute-done.12, bf16[512,1152]{0,1:T(8,128)(2,1)} %copy-done.13, f32[]{:T(128)} %bitcast.178, f32[]{:T(128)} %bitcast.170), kind=kOutput, calls=%fused_computation.1 | convolution fusion | flops 1210384384 | bytes 7077896 | tf_op jit(solution)/shard_map/dot_general | solution.py:120
  158.4 6.1 %convolution_add_fusion.4 = f32[512,1152]{0,1:T(8,128)} fusion(f32[512,1152]{0,1:T(8,128)} %convolution_add_fusion.5, bf16[512,1152]{0,1:T(8,128)(2,1)} %collective-permute-done.9, bf16[512,1152]{0,1:T(8,128)(2,1)} %copy-done.10, f32[]{:T(128)} %bitcast.181, f32[]{:T(128)} %bitcast.171), kind=kOutput, calls=%fused_computation.4 | convolution fusion | flops 1210384384 | bytes 7077896 | tf_op jit(solution)/shard_map/dot_general | solution.py:119
  164.5 31.3 %collective-permute-done.13 = bf16[512,1152]{0,1:T(8,128)(2,1)} collective-permute-done((bf16[512,1152]{0,1:T(8,128)(2,1)}, bf16[512,1152]{0,1:T(8,128)(2,1)}, u32[]{:S(2)}, u32[]{:S(2)}) %collective-permute-start.13) | collective-permute-done | bytes 1179680 | tf_op jit(solution)/shard_map/ppermute | solution.py:12
  195.8 6.6 %fusion.12 = (f32[512]{0:T(512)S(1)}, f32[512,1152]{0,1:T(8,128)}) fusion(f32[1152,512]{1,0:T(8,128)} %copy-done.9, f32[512]{0:T(512)S(1)} %add_rsqrt_fusion, f32[512,1152]{0,1:T(8,128)} %convolution_add_fusion.1, bf16[512,1152]{0,1:T(8,128)(2,1)} %collective-permute-done.13, bf16[512,1152]{0,1:T(8,128)(2,1)} %copy-done.13, f32[]{:T(128)} %bitcast.177, ...), kind=kOutput, calls=%fused_computation.29 | convolution fusion | flops 1212153344 | bytes 9441288 | tf_op jit(solution)/shard_map/dot_general | solution.py:120
  202.4 3.0 fusion.15
  207.3 2.0 fusion.1
  209.3 2.6 copy.45
  211.9 3.1 fusion.3
  214.9 2.6 copy.49
  217.5 2.7 slice_bitcast_fusion.6
  222.0 5.6 %fusion.16 = (f32[512]{0:T(512)S(1)}, f32[512,1152]{0,1:T(8,128)}) fusion(f32[1152,512]{1,0:T(8,128)S(1)} %get-tuple-element.79, f32[512]{0:T(512)S(1)} %add_rsqrt_fusion.1, f32[512,1152]{0,1:T(8,128)} %convolution_add_fusion.4, bf16[512,1152]{0,1:T(8,128)(2,1)} %collective-permute-done.10, bf16[512,1152]{0,1:T(8,128)(2,1)S(1)} %copy-done.11, ...), kind=kOutput, calls=%fused_computation.36 | convolution fusion | flops 1212153344 | bytes 9441288 | tf_op jit(solution)/shard_map/dot_general | solution.py:119
  227.6 2.3 fusion.19
  234.9 2.0 fusion.2
  236.9 2.1 copy.47
  247.6 1.5 copy-done.2
  251.6 13.5 %collective-permute-done.20 = bf16[2,2,144,576]{3,2,0,1:T(8,128)(2,1)} collective-permute-done((bf16[2,2,144,576]{3,2,0,1:T(8,128)(2,1)}, bf16[2,2,144,576]{3,2,0,1:T(8,128)(2,1)}, u32[]{:S(2)}, u32[]{:S(2)}) %collective-permute-start.20) | collective-permute-done | bytes 663584 | tf_op jit(solution)/shard_map/ppermute | solution.py:17
  266.7 1.5 collective-permute-start.21
  271.9 4.9 %collective-permute-done.21 = bf16[2,144,576]{2,1,0:T(8,128)(2,1)S(1)} collective-permute-done((bf16[2,144,576]{2,1,0:T(8,128)(2,1)S(1)}, bf16[2,144,576]{2,1,0:T(8,128)(2,1)S(1)}, u32[]{:S(2)}, u32[]{:S(2)}) %collective-permute-start.21) | collective-permute-done | bytes 331808 | tf_op jit(solution)/shard_map/ppermute | solution.py:17
  277.0 2.6 collective-permute-start.22
  280.5 2.6 collective-permute-start.17
  283.1 9.1 %collective-permute-done.22 = bf16[144,576]{1,0:T(8,128)(2,1)S(1)} collective-permute-done((bf16[144,576]{1,0:T(8,128)(2,1)S(1)}, bf16[144,576]{1,0:T(8,128)(2,1)S(1)}, u32[]{:S(2)}, u32[]{:S(2)}) %collective-permute-start.22) | collective-permute-done | bytes 165920 | tf_op jit(solution)/shard_map/ppermute | solution.py:17
  292.4 2.7 collective-permute-done.17
  295.8 2.1 collective-permute-done.23
  297.9 2.2 collective-permute-done.18
  301.5 2.2 collective-permute-start.24
  304.4 7.5 %collective-permute-done.24 = bf16[1,144,288]{2,1,0:T(8,128)(2,1)S(1)} collective-permute-done((bf16[1,144,288]{2,1,0:T(8,128)(2,1)S(1)}, bf16[1,144,288]{2,1,0:T(8,128)(2,1)S(1)}, u32[]{:S(2)}, u32[]{:S(2)}) %collective-permute-start.24) | collective-permute-done | bytes 82976 | tf_op jit(solution)/shard_map/ppermute | solution.py:17
  314.3 6.0 %collective-permute-done.25 = bf16[2,144,288]{2,1,0:T(8,128)(2,1)S(1)} collective-permute-done((bf16[2,144,288]{2,1,0:T(8,128)(2,1)S(1)}, bf16[2,144,288]{2,1,0:T(8,128)(2,1)S(1)}, u32[]{:S(2)}, u32[]{:S(2)}) %collective-permute-start.25) | collective-permute-done | bytes 165920 | tf_op jit(solution)/shard_map/ppermute | solution.py:17
  321.2 2.0 collective-permute-start.26
  330.1 3.7 %collective-permute-done.26 = bf16[4,144,288]{2,1,0:T(8,128)(2,1)} collective-permute-done((bf16[4,144,288]{2,1,0:T(8,128)(2,1)}, bf16[4,144,288]{2,1,0:T(8,128)(2,1)}, u32[]{:S(2)}, u32[]{:S(2)}) %collective-permute-start.26) | collective-permute-done | bytes 331808 | tf_op jit(solution)/shard_map/ppermute | solution.py:17
  333.9 4.7 %collective-permute-done.29 = bf16[4,144,288]{2,1,0:T(8,128)(2,1)} collective-permute-done((bf16[4,144,288]{2,1,0:T(8,128)(2,1)}, bf16[4,144,288]{2,1,0:T(8,128)(2,1)}, u32[]{:S(2)}, u32[]{:S(2)}) %collective-permute-start.29) | collective-permute-done | bytes 331808 | tf_op jit(solution)/shard_map/ppermute | solution.py:17
  (155 shorter events, 54.3 us)
Async XLA Ops:
  0.6 31.4 %copy-start = (bf16[512,1152]{1,0:T(8,128)(2,1)S(1)}, bf16[512,1152]{1,0:T(8,128)(2,1)}, u32[]{:S(2)}) copy-start(bf16[512,1152]{1,0:T(8,128)(2,1)} %param.9) | copy-start | bytes 3538948
  0.6 15.4 %copy-start.4 = (bf16[288,2304]{1,0:T(8,128)(2,1)S(1)}, bf16[288,2304]{1,0:T(8,128)(2,1)}, u32[]{:S(2)}) copy-start(bf16[288,2304]{1,0:T(8,128)(2,1)} %param.10) | copy-start | bytes 3981316
  2.2 11.7 %collective-permute-start.4 = (bf16[144,1152]{1,0:T(8,128)(2,1)S(1)}, bf16[144,1152]{1,0:T(8,128)(2,1)}, u32[]{:S(2)}, u32[]{:S(2)}) collective-permute-start(bf16[144,1152]{1,0:T(8,128)(2,1)S(1)} %get-tuple-element.53), channel_id=1, source_target_pairs={{0,2},{1,3},{2,0},{3,1},{4,6},{5,7},{6,4},{7,5},{8,10},{9,11},{10,... | collective-permute-start | bytes 995336 | tf_op jit(solution)/shard_map/ppermute | solution.py:17
  5.2 15.0 %collective-permute-start = (bf16[144,1152]{1,0:T(8,128)(2,1)S(1)}, bf16[144,1152]{1,0:T(8,128)(2,1)}, u32[]{:S(2)}, u32[]{:S(2)}) collective-permute-start(bf16[144,1152]{1,0:T(8,128)(2,1)S(1)} %get-tuple-element.54), channel_id=1, source_target_pairs={{0,2},{1,3},{2,0},{3,1},{4,6},{5,7},{6,4},{7,5},{8,10},{9,11},{10,... | collective-permute-start | bytes 995336 | tf_op jit(solution)/shard_map/ppermute | solution.py:17
  13.9 8.5 %collective-permute-start.5 = (bf16[144,1152]{1,0:T(8,128)(2,1)}, bf16[144,1152]{1,0:T(8,128)(2,1)}, u32[]{:S(2)}, u32[]{:S(2)}) collective-permute-start(bf16[144,1152]{1,0:T(8,128)(2,1)} %collective-permute-done.4), channel_id=1, source_target_pairs={{0,4},{4,0},{8,12},{12,8},{16,20},{20,16},{24,28},{28,24},{1,5},{5... | collective-permute-start | bytes 995336 | tf_op jit(solution)/shard_map/ppermute | solution.py:17
  16.9 13.7 %collective-permute-start.7 = (bf16[288,1152]{1,0:T(8,128)(2,1)}, bf16[288,1152]{1,0:T(8,128)(2,1)S(1)}, u32[]{:S(2)}, u32[]{:S(2)}) collective-permute-start(bf16[288,1152]{1,0:T(8,128)(2,1)} %slice.141), channel_id=1, source_target_pairs={{0,1},{1,0},{2,3},{3,2},{4,5},{5,4},{6,7},{7,6},{8,9},{9,8},{10,11... | collective-permute-start | bytes 1990664 | tf_op jit(solution)/shard_map/ppermute | solution.py:17
  20.2 9.2 %collective-permute-start.1 = (bf16[144,1152]{1,0:T(8,128)(2,1)}, bf16[144,1152]{1,0:T(8,128)(2,1)S(1)}, u32[]{:S(2)}, u32[]{:S(2)}) collective-permute-start(bf16[144,1152]{1,0:T(8,128)(2,1)} %collective-permute-done), channel_id=1, source_target_pairs={{0,4},{4,0},{8,12},{12,8},{16,20},{20,16},{24,28},{28,24},{1,5},{5... | collective-permute-start | bytes 995336 | tf_op jit(solution)/shard_map/ppermute | solution.py:17
  23.6 7.7 %collective-permute-start.6 = (bf16[288,1152]{1,0:T(8,128)(2,1)S(1)}, bf16[288,1152]{1,0:T(8,128)(2,1)S(1)}, u32[]{:S(2)}, u32[]{:S(2)}) collective-permute-start(bf16[288,1152]{1,0:T(8,128)(2,1)S(1)} %pad_maximum_fusion.10), channel_id=1, source_target_pairs={{0,1},{1,0},{2,3},{3,2},{4,5},{5,4},{6,7},{7,6},{8,9},{9,8},{10,11... | collective-permute-start | bytes 1990664 | tf_op jit(solution)/shard_map/ppermute | solution.py:17
  30.5 3.4 collective-permute-start.2
  30.7 3.4 collective-permute-start.3
  33.8 8.7 %copy-start.9 = (f32[1152,512]{1,0:T(8,128)}, f32[1152,512]{1,0:T(8,128)S(1)}, u32[]{:S(2)}) copy-start(f32[1152,512]{1,0:T(8,128)S(1)} %get-tuple-element.81) | copy-start | bytes 7077892
  38.0 55.8 %copy-start.10 = (bf16[512,1152]{0,1:T(8,128)(2,1)}, bf16[512,1152]{0,1:T(8,128)(2,1)S(1)}, u32[]{:S(2)}) copy-start(bf16[512,1152]{0,1:T(8,128)(2,1)S(1)} %bitcast_convert_fusion.1) | copy-start | bytes 3538948
  38.0 53.3 %collective-permute-start.11 = (bf16[512,1152]{0,1:T(8,128)(2,1)S(1)}, bf16[512,1152]{0,1:T(8,128)(2,1)}, u32[]{:S(2)}, u32[]{:S(2)}) collective-permute-start(bf16[512,1152]{0,1:T(8,128)(2,1)S(1)} %bitcast_convert_fusion.1), channel_id=1, source_target_pairs={{0,28},{4,0},{8,4},{12,8},{16,12},{20,16},{24,20},{28,24},{1,29},{... | collective-permute-start | bytes 3538952 | tf_op jit(solution)/shard_map/ppermute | solution.py:12
  42.9 53.1 %copy-start.13 = (bf16[512,1152]{0,1:T(8,128)(2,1)}, bf16[512,1152]{0,1:T(8,128)(2,1)S(1)}, u32[]{:S(2)}) copy-start(bf16[512,1152]{0,1:T(8,128)(2,1)S(1)} %bitcast_convert_fusion) | copy-start | bytes 3538948
  42.9 53.1 %collective-permute-start.8 = (bf16[512,1152]{0,1:T(8,128)(2,1)S(1)}, bf16[512,1152]{0,1:T(8,128)(2,1)}, u32[]{:S(2)}, u32[]{:S(2)}) collective-permute-start(bf16[512,1152]{0,1:T(8,128)(2,1)S(1)} %bitcast_convert_fusion), channel_id=1, source_target_pairs={{0,4},{4,8},{8,12},{12,16},{16,20},{20,24},{24,28},{28,0},{1,5},{5... | collective-permute-start | bytes 3538952 | tf_op jit(solution)/shard_map/ppermute | solution.py:12
  91.4 52.7 %collective-permute-start.12 = (bf16[512,1152]{0,1:T(8,128)(2,1)}, bf16[512,1152]{0,1:T(8,128)(2,1)}, u32[]{:S(2)}, u32[]{:S(2)}) collective-permute-start(bf16[512,1152]{0,1:T(8,128)(2,1)} %collective-permute-done.11), channel_id=1, source_target_pairs={{0,28},{4,0},{8,4},{12,8},{16,12},{20,16},{24,20},{28,24},{1,29},{... | collective-permute-start | bytes 3538952 | tf_op jit(solution)/shard_map/ppermute | solution.py:12
  96.0 56.5 %collective-permute-start.9 = (bf16[512,1152]{0,1:T(8,128)(2,1)}, bf16[512,1152]{0,1:T(8,128)(2,1)}, u32[]{:S(2)}, u32[]{:S(2)}) collective-permute-start(bf16[512,1152]{0,1:T(8,128)(2,1)} %collective-permute-done.8), channel_id=1, source_target_pairs={{0,4},{4,8},{8,12},{12,16},{16,20},{20,24},{24,28},{28,0},{1,5},{5... | collective-permute-start | bytes 3538952 | tf_op jit(solution)/shard_map/ppermute | solution.py:12
  144.0 51.7 %collective-permute-start.13 = (bf16[512,1152]{0,1:T(8,128)(2,1)}, bf16[512,1152]{0,1:T(8,128)(2,1)}, u32[]{:S(2)}, u32[]{:S(2)}) collective-permute-start(bf16[512,1152]{0,1:T(8,128)(2,1)} %collective-permute-done.12), channel_id=1, source_target_pairs={{0,28},{4,0},{8,4},{12,8},{16,12},{20,16},{24,20},{28,24},{1,29},{... | collective-permute-start | bytes 3538952 | tf_op jit(solution)/shard_map/ppermute | solution.py:12
  152.5 69.0 %collective-permute-start.10 = (bf16[512,1152]{0,1:T(8,128)(2,1)}, bf16[512,1152]{0,1:T(8,128)(2,1)}, u32[]{:S(2)}, u32[]{:S(2)}) collective-permute-start(bf16[512,1152]{0,1:T(8,128)(2,1)} %collective-permute-done.9), channel_id=1, source_target_pairs={{0,4},{4,8},{8,12},{12,16},{16,20},{20,24},{24,28},{28,0},{1,5},{5... | collective-permute-start | bytes 3538952 | tf_op jit(solution)/shard_map/ppermute | solution.py:12
  217.5 2.7 copy-start.12
  220.2 1.8 copy-start.11
  241.4 3.3 collective-permute-start.19
  243.8 3.3 collective-permute-start.14
  246.3 18.8 %collective-permute-start.20 = (bf16[2,2,144,576]{3,2,0,1:T(8,128)(2,1)}, bf16[2,2,144,576]{3,2,0,1:T(8,128)(2,1)}, u32[]{:S(2)}, u32[]{:S(2)}) collective-permute-start(bf16[2,2,144,576]{3,2,0,1:T(8,128)(2,1)} %fusion.76), channel_id=1, source_target_pairs={{0,4},{4,0},{8,12},{12,8},{16,20},{20,16},{24,28},{28,24},{1,5},{5... | collective-permute-start | bytes 1990664 | tf_op jit(solution)/shard_map/ppermute | solution.py:17
  250.2 19.1 %collective-permute-start.15 = (bf16[2,2,144,576]{3,2,1,0:T(8,128)(2,1)}, bf16[2,2,144,576]{3,2,1,0:T(8,128)(2,1)}, u32[]{:S(2)}, u32[]{:S(2)}) collective-permute-start(bf16[2,2,144,576]{3,2,1,0:T(8,128)(2,1)} %fusion.75), channel_id=1, source_target_pairs={{0,2},{1,3},{2,0},{3,1},{4,6},{5,7},{6,4},{7,5},{8,10},{9,11},{10,... | collective-permute-start | bytes 1990664 | tf_op jit(solution)/shard_map/ppermute | solution.py:17
  265.1 4.1 %copy-start.3 = (f32[2,2,2,144,576]{4,3,2,1,0:T(8,128)S(1)}, f32[2,2,2,144,576]{4,3,2,1,0:T(8,128)}, u32[]{:S(2)}) copy-start(f32[2,2,2,144,576]{4,3,2,1,0:T(8,128)} %copy-done.2) | copy-start | bytes 7962628
  266.7 10.2 %collective-permute-start.21 = (bf16[2,144,576]{2,1,0:T(8,128)(2,1)S(1)}, bf16[2,144,576]{2,1,0:T(8,128)(2,1)S(1)}, u32[]{:S(2)}, u32[]{:S(2)}) collective-permute-start(bf16[2,144,576]{2,1,0:T(8,128)(2,1)S(1)} %fusion.96), channel_id=1, source_target_pairs={{0,2},{1,3},{2,0},{3,1},{4,6},{5,7},{6,4},{7,5},{8,10},{9,11},{10,... | collective-permute-start | bytes 995336 | tf_op jit(solution)/shard_map/ppermute | solution.py:17
  270.6 9.6 %collective-permute-start.16 = (bf16[2,144,576]{2,1,0:T(8,128)(2,1)S(1)}, bf16[2,144,576]{2,1,0:T(8,128)(2,1)S(1)}, u32[]{:S(2)}, u32[]{:S(2)}) collective-permute-start(bf16[2,144,576]{2,1,0:T(8,128)(2,1)S(1)} %fusion.95), channel_id=1, source_target_pairs={{0,4},{4,0},{8,12},{12,8},{16,20},{20,16},{24,28},{28,24},{1,5},{5... | collective-permute-start | bytes 995336 | tf_op jit(solution)/shard_map/ppermute | solution.py:17
  277.0 15.2 %collective-permute-start.22 = (bf16[144,576]{1,0:T(8,128)(2,1)S(1)}, bf16[144,576]{1,0:T(8,128)(2,1)S(1)}, u32[]{:S(2)}, u32[]{:S(2)}) collective-permute-start(bf16[144,576]{1,0:T(8,128)(2,1)S(1)} %fusion.100), channel_id=1, source_target_pairs={{0,16},{4,20},{8,24},{12,28},{16,0},{20,4},{24,8},{28,12},{1,17},{... | collective-permute-start | bytes 497672 | tf_op jit(solution)/shard_map/ppermute | solution.py:17
  280.4 19.6 %copy-start.23 = (f32[288,288]{1,0:T(8,128)S(1)}, f32[288,288]{1,0:T(8,128)}, u32[]{:S(2)}) copy-start(f32[288,288]{1,0:T(8,128)} %param.13) | copy-start | bytes 995332
  280.5 19.6 %copy-start.24 = (f32[288,288]{1,0:T(8,128)S(1)}, f32[288,288]{1,0:T(8,128)}, u32[]{:S(2)}) copy-start(f32[288,288]{1,0:T(8,128)} %param.15) | copy-start | bytes 995332
  280.5 19.6 %copy-start.25 = (f32[288,288]{1,0:T(8,128)S(1)}, f32[288,288]{1,0:T(8,128)}, u32[]{:S(2)}) copy-start(f32[288,288]{1,0:T(8,128)} %param.14) | copy-start | bytes 995332
  280.5 14.6 %collective-permute-start.17 = (bf16[144,576]{1,0:T(8,128)(2,1)S(1)}, bf16[144,576]{1,0:T(8,128)(2,1)S(1)}, u32[]{:S(2)}, u32[]{:S(2)}) collective-permute-start(bf16[144,576]{1,0:T(8,128)(2,1)S(1)} %fusion.99), channel_id=1, source_target_pairs={{0,16},{4,20},{8,24},{12,28},{16,0},{20,4},{24,8},{28,12},{1,17},{... | collective-permute-start | bytes 497672 | tf_op jit(solution)/shard_map/ppermute | solution.py:17
  292.3 5.6 %collective-permute-start.23 = (bf16[144,288]{1,0:T(8,128)(2,1)S(1)}, bf16[144,288]{1,0:T(8,128)(2,1)S(1)}, u32[]{:S(2)}, u32[]{:S(2)}) collective-permute-start(bf16[144,288]{1,0:T(8,128)(2,1)S(1)} %select_convert_fusion.6), channel_id=1, source_target_pairs={{0,8},{4,12},{8,0},{12,4},{16,24},{20,28},{24,16},{28,20},{1,9},{5... | collective-permute-start | bytes 248840 | tf_op jit(solution)/shard_map/ppermute | solution.py:17
  295.3 4.8 %collective-permute-start.18 = (bf16[144,288]{1,0:T(8,128)(2,1)S(1)}, bf16[144,288]{1,0:T(8,128)(2,1)S(1)}, u32[]{:S(2)}, u32[]{:S(2)}) collective-permute-start(bf16[144,288]{1,0:T(8,128)(2,1)S(1)} %select_convert_fusion.7), channel_id=1, source_target_pairs={{0,8},{4,12},{8,0},{12,4},{16,24},{20,28},{24,16},{28,20},{1,9},{5... | collective-permute-start | bytes 248840 | tf_op jit(solution)/shard_map/ppermute | solution.py:17
  301.5 10.4 %collective-permute-start.24 = (bf16[1,144,288]{2,1,0:T(8,128)(2,1)S(1)}, bf16[1,144,288]{2,1,0:T(8,128)(2,1)S(1)}, u32[]{:S(2)}, u32[]{:S(2)}) collective-permute-start(bf16[1,144,288]{2,1,0:T(8,128)(2,1)S(1)} %get-tuple-element.18), channel_id=1, source_target_pairs={{0,16},{4,20},{8,24},{12,28},{16,0},{20,4},{24,8},{28,12},{1,17},{... | collective-permute-start | bytes 248840 | tf_op jit(solution)/shard_map/ppermute | solution.py:17
  303.7 9.6 %collective-permute-start.27 = (bf16[1,144,288]{2,1,0:T(8,128)(2,1)S(1)}, bf16[1,144,288]{2,1,0:T(8,128)(2,1)S(1)}, u32[]{:S(2)}, u32[]{:S(2)}) collective-permute-start(bf16[1,144,288]{2,1,0:T(8,128)(2,1)S(1)} %get-tuple-element.47), channel_id=1, source_target_pairs={{0,16},{4,20},{8,24},{12,28},{16,0},{20,4},{24,8},{28,12},{1,17},{... | collective-permute-start | bytes 248840 | tf_op jit(solution)/shard_map/ppermute | solution.py:17
  312.0 8.2 %collective-permute-start.25 = (bf16[2,144,288]{2,1,0:T(8,128)(2,1)S(1)}, bf16[2,144,288]{2,1,0:T(8,128)(2,1)S(1)}, u32[]{:S(2)}, u32[]{:S(2)}) collective-permute-start(bf16[2,144,288]{2,1,0:T(8,128)(2,1)S(1)} %pad_maximum_fusion.16), channel_id=1, source_target_pairs={{0,8},{4,12},{8,0},{12,4},{16,24},{20,28},{24,16},{28,20},{1,9},{5... | collective-permute-start | bytes 497672 | tf_op jit(solution)/shard_map/ppermute | solution.py:17
  313.3 9.8 %collective-permute-start.28 = (bf16[2,144,288]{2,1,0:T(8,128)(2,1)S(1)}, bf16[2,144,288]{2,1,0:T(8,128)(2,1)S(1)}, u32[]{:S(2)}, u32[]{:S(2)}) collective-permute-start(bf16[2,144,288]{2,1,0:T(8,128)(2,1)S(1)} %pad_maximum_fusion.17), channel_id=1, source_target_pairs={{0,8},{4,12},{8,0},{12,4},{16,24},{20,28},{24,16},{28,20},{1,9},{5... | collective-permute-start | bytes 497672 | tf_op jit(solution)/shard_map/ppermute | solution.py:17
  320.3 5.2 %copy-start.6 = (bf16[512,1152]{0,1:T(8,128)(2,1)S(1)}, bf16[512,1152]{0,1:T(8,128)(2,1)}, u32[]{:S(2)}) copy-start(bf16[512,1152]{0,1:T(8,128)(2,1)} %copy-done.5) | copy-start | bytes 3538948
  321.2 12.7 %collective-permute-start.26 = (bf16[4,144,288]{2,1,0:T(8,128)(2,1)}, bf16[4,144,288]{2,1,0:T(8,128)(2,1)}, u32[]{:S(2)}, u32[]{:S(2)}) collective-permute-start(bf16[4,144,288]{2,1,0:T(8,128)(2,1)} %pad_maximum_fusion.14), channel_id=1, source_target_pairs={{0,4},{4,0},{8,12},{12,8},{16,20},{20,16},{24,28},{28,24},{1,5},{5... | collective-permute-start | bytes 995336 | tf_op jit(solution)/shard_map/ppermute | solution.py:17
  323.2 3.7 %copy-start.8 = (bf16[512,1152]{0,1:T(8,128)(2,1)S(1)}, bf16[512,1152]{0,1:T(8,128)(2,1)}, u32[]{:S(2)}) copy-start(bf16[512,1152]{0,1:T(8,128)(2,1)} %copy-done.7) | copy-start | bytes 3538948
  324.1 14.5 %collective-permute-start.29 = (bf16[4,144,288]{2,1,0:T(8,128)(2,1)}, bf16[4,144,288]{2,1,0:T(8,128)(2,1)}, u32[]{:S(2)}, u32[]{:S(2)}) collective-permute-start(bf16[4,144,288]{2,1,0:T(8,128)(2,1)} %pad_maximum_fusion.15), channel_id=1, source_target_pairs={{0,4},{4,0},{8,12},{12,8},{16,20},{20,16},{24,28},{28,24},{1,5},{5... | collective-permute-start | bytes 995336 | tf_op jit(solution)/shard_map/ppermute | solution.py:17
  326.9 2.2 copy-start.19
  326.9 2.2 copy-start.20
  326.9 2.2 copy-start.21
  327.0 2.2 copy-start.22
  342.8 1.8 copy-start.1
  (11 other events, 14.6 us)
